TPU v7x, 256 devices: a whole 4x4x8 slice. The times are simulated.
256 devices in a mesh: row: 16 (over x_hi, z), col: 16 (over x_lo, y, core).
Axes of the slice: x: 4 (x_hi: 2, x_lo: 2; x = x_hi * 2 + x_lo), y: 4, z: 8, core: 2. Of those that a mesh axis runs over, the one named last changes fastest.
Arguments:
- inputs: bfloat16 [1536, 12288], P('col', 'row'), may hold values from -6 to 6
- grad_out: bfloat16 [1536, 49152], P('row', 'col'), may hold values from -6 to 6
- weight: bfloat16 [12288, 49152], P('row', 'col'), may hold values from -0.02734375 to 0.02734375
Outputs:
- weight_grad: bfloat16 [12288, 49152], P('row', 'col')
- input_grad: bfloat16 [1536, 12288], P('col', 'row')
All inputs are finite; a program needn't handle non-finite values.
Results may differ from a plain program's by a relative error of at most 0.001.
Values may be sent and summed in bfloat16 or wider, within the bound.
No kernel may reach another device: no remote copies, remote signals or barrier semaphores. Data moves between devices by JAX's collectives and lax.ppermute only.
A program may use at most 64 MiB of HBM per device.

v0:
```python
import jax
import jax.numpy as jnp
from jax import lax
from jax.sharding import PartitionSpec as P


def body(inputs, grad_out, weight):
    all_inputs = lax.all_gather(inputs, "col", axis=0, tiled=True)
    all_grads = None
    partial_value = None
    all_grads = lax.all_gather(grad_out, "row", axis=0, tiled=True)
    weight_acc = lax.dot_general(
        all_inputs, all_grads, (((0,), (0,)), ((), ())), preferred_element_type=jnp.float32
    )
    partial_value = lax.dot_general(
        all_grads, weight, (((1,), (1,)), ((), ())), preferred_element_type=jnp.float32
    )
    summed = lax.psum_scatter(partial_value, "col", scatter_dimension=0, tiled=True)
    return (weight_acc.astype(jnp.bfloat16), summed.astype(jnp.bfloat16))


def solution(mesh):
    in_specs = (P("col", "row"), P("row", "col"), P("row", "col"))
    out_specs = (P("row", "col"), P("col", "row"))
    return jax.shard_map(body, mesh=mesh, in_specs=in_specs, out_specs=out_specs, check_vma=False)
```

profile of v0, /device:TPU:1, one launch (start us, length us, event | category | flops | bytes accessed | tf_op | source)
XLA Modules:
  0.0 273.9 jit_solution(18125615488951149930)
XLA Ops:
  7.2 0.0 all-gather.5.cloned.1.call-start
  7.2 0.7 all-gather.5.cloned.1.call-update
  7.9 0.0 all-gather.3.cloned.1.call-start
  7.9 0.7 all-gather.3.cloned.1.call-update
  8.6 0.0 reduce-scatter.2.cloned.1.call-start
  8.7 151.6 %all-gather.5.cloned.1.call-done = bf16[1536,3072]{1,0:T(8,128)(2,1)} async-done(((bf16[96,3072]{1,0:T(8,128)(2,1)}), bf16[1536,3072]{1,0:T(8,128)(2,1)}) %all-gather.5.cloned.1.call-update) | async-done | bytes 9437200 | tf_op jit(solution)/shard_map/all_gather | solution.py:11
  160.3 13.0 %fusion = f32[1536,768]{1,0:T(8,128)} fusion(bf16[1536,3072]{1,0:T(8,128)(2,1)} %all-gather.5.cloned.1.call-done, bf16[768,3072]{1,0:T(8,128)(2,1)} %param.5), kind=kOutput, calls=%fused_computation.1 | convolution fusion | flops 7247757312 | bytes 18874368 | tf_op jit(solution)/shard_map/dot_general | solution.py:15
  173.3 0.0 reduce-scatter.2.cloned.1.call-update
  173.4 23.4 %all-gather.3.cloned.1.call-done = bf16[1536,768]{1,0:T(8,128)(2,1)} async-done(((bf16[96,768]{1,0:T(8,128)(2,1)}), bf16[1536,768]{1,0:T(8,128)(2,1)}) %all-gather.3.cloned.1.call-update) | async-done | bytes 2359312 | tf_op jit(solution)/shard_map/all_gather | solution.py:8
  196.8 12.3 %convolution_convert_fusion = bf16[768,3072]{1,0:T(8,128)(2,1)} fusion(bf16[1536,768]{1,0:T(8,128)(2,1)} %all-gather.3.cloned.1.call-done, bf16[1536,3072]{1,0:T(8,128)(2,1)} %all-gather.5.cloned.1.call-done), kind=kOutput, calls=%fused_computation | convolution fusion | flops 7250116608 | bytes 16515072 | tf_op jit(solution)/shard_map/dot_general | solution.py:12
  209.0 56.7 %reduce-scatter.2.cloned.1.call-done = f32[96,768]{1,0:T(8,128)} async-done(((f32[1536,768]{1,0:T(8,128)}), f32[96,768]{1,0:T(8,128)}) %reduce-scatter.2.cloned.1.call-update) | async-done | bytes 294928 | tf_op jit(solution)/shard_map/reduce_scatter | solution.py:18
  265.7 1.6 convert_element_type.7
Async XLA Ops:
  7.2 153.2 %all-gather.5.cloned.1.call-start = ((), (), s32[]{:S(2)}) async-start(), calls=%async_computation.2 | async-start | bytes 10027008 | tf_op jit(solution)/shard_map/all_gather | solution.py:11
  7.9 188.9 %all-gather.3.cloned.1.call-start = ((), (), s32[]{:S(2)}) async-start(), calls=%async_computation.1 | async-start | bytes 2506752 | tf_op jit(solution)/shard_map/all_gather | solution.py:8
  8.6 257.1 %reduce-scatter.2.cloned.1.call-start = ((), (), s32[]{:S(2)}) async-start(), calls=%async_computation.3 | async-start | bytes 5013504 | tf_op jit(solution)/shard_map/reduce_scatter | solution.py:18
Sparse Core Ops, SparseCore 0:
  10.6 149.6 all-gather.4
  162.2 34.5 all-gather.2
  199.3 66.3 reduce-scatter.1
where the time goes:
time: 277 us; the launch traced here: 274 us
  waiting for transfers between devices  233 us (84%)
  matrix products  25.3 us (9%)
  between operations  13.7 us (5%)
    all_gather x1, waiting for transfers between devices, body(): all_grads = lax.all_gather(grad_out, 'row', axis=0, tiled=True)  152 us
    reduce_scatter x1, waiting for transfers between devices, body(): lax.psum_scatter(partial_value, 'col', scatter_dimension=0, tiled=True)  56.7 us
    all_gather x1, waiting for transfers between devices, body(): all_inputs = lax.all_gather(inputs, 'col', axis=0, tiled=True)  23.4 us
    dot_general x1, matrix products, body(): lax.dot_general(all_grads, weight, (((1,), (1,)), ((), ())), preferred_el...  13 us
    dot_general x1, matrix products, body(): lax.dot_general(all_inputs, all_grads, (((0,), (0,)), ((), ())), preferre...  12.3 us
  transfers between devices with their start and end apart: 3, of which 3 were waited for; matrix products, arithmetic and copies ran while one was open for 9% of the time, Pallas kernels for 0%

commit v1 on v0

v1 whole, which is shorter than its diff:
```python
import jax
import jax.numpy as jnp
from jax import lax
from jax.experimental import pallas as pl
from jax.experimental.pallas import tpu as pltpu
from jax.sharding import PartitionSpec as P

BF16, F32 = jnp.bfloat16, jnp.float32
ARRIVAL = (0, 1, -1, -2, 2, 3, -3, -4)
GROUPS = {"late": (0, 48), "first": (48, 96)}
ORDER = "AbBabBfabBfabBfafB"
IN_FLIGHT = 4
INPUT_TILE, WEIGHT_TILE, VMEM_LIMIT = 768, 512, 40 << 20


def by_row(move):
    return [(r, move(r // 8, r % 8)) for r in range(16)]


def by_col(move):
    def target(c):
        x, y, core = move(c // 8, (c // 2) % 4, c % 2)
        return x * 8 + (y % 4) * 2 + core

    return [(c, target(c)) for c in range(16)]


def z_pairs(second):
    pairs = []
    for r in range(16):
        for c in range(16):
            z = r % 8
            up = (z + c + second) % 2 == 0
            other = (r // 8) * 8 + (z + (1 if up else -1)) % 8
            pairs.append((r * 16 + c, other * 16 + c))
    return pairs


X_FAR = by_row(lambda x, z: (1 - x) * 8 + z)
OTHER_CORE = by_col(lambda x, y, k: (x, y, 1 - k))
Z_FIRST, Z_SECOND = z_pairs(0), z_pairs(1)
SAME_CORE = [[c for c in range(16) if c % 2 == k] for k in range(2)]


class Lane:
    def __init__(self):
        self.sent = []

    def after(self, value):
        if len(self.sent) >= IN_FLIGHT:
            value, _ = lax.optimization_barrier((value, self.sent[-IN_FLIGHT]))
        return value

    def send(self, value, axis, pairs):
        out = lax.ppermute(self.after(value), axis, pairs)
        self.sent.append(out)
        return out


class Ring:
    def __init__(self, lane, block):
        self.lane, self.got = lane, [block[None]]

    def step(self):
        at = len(self.got)
        payload = jnp.concatenate(self.got, 0) if at == 2 else self.got[-1]
        pairs = Z_FIRST if at % 2 else Z_SECOND
        self.got.append(self.lane.send(payload, ("row", "col"), pairs))


class Place:
    def __init__(self):
        row, col = lax.axis_index("row"), lax.axis_index("col")
        self.x, self.z, self.core = row // 8, row % 8, col % 2
        self.sign = 1 - 2 * ((self.z + col) % 2)

    def rows(self, x_major):
        order = [(f, d) for f in (0, 1) for d in ARRIVAL]
        if not x_major:
            order = [(f, d) for d in ARRIVAL for f in (0, 1)]
        return [((self.x + f) % 2) * 8 + (self.z + self.sign * d + 8) % 8 for f, d in order]


def input_grad_parts(pieces, weight, place, spans):
    n, width, depth = len(pieces), weight.shape[1], weight.shape[0]
    steps = width // INPUT_TILE
    tokens = sum(p.shape[0] for p in pieces)
    where = [(r % 2, r // 2) for r in place.rows(True)]
    keep = jnp.stack([jnp.where(core == place.core, 1, 0) for core, _ in where])
    slot = jnp.stack([at for _, at in where])

    def kernel(keep_ref, slot_ref, *refs):
        piece_refs, weight_ref, mine_ref, other_ref, total = refs[:n], refs[n], refs[n + 1], refs[n + 2], refs[n + 3]
        step = pl.program_id(0)
        block = jnp.concatenate([ref[...] for ref in piece_refs], 0)
        product = dot(block, weight_ref[...], ((1,), (1,)))

        @pl.when(step == 0)
        def _():
            total[...] = product

        @pl.when(step > 0)
        def _():
            total[...] += product

        @pl.when(step == steps - 1)
        def _():
            at = 0
            for index, (first, last) in enumerate(spans):
                found = slice(at, at + last - first)
                at += last - first
                for ref, wanted in ((mine_ref, 1), (other_ref, 0)):

                    @pl.when(keep_ref[index % 16] == wanted)
                    def _():
                        ref[slot_ref[index % 16], first:last] = total[found]

    rows = tokens // 16
    half = jax.ShapeDtypeStruct((8, rows, depth), F32)
    whole = pl.BlockSpec((8, rows, depth), lambda k, *_: (0, 0, 0))
    return pl.pallas_call(
        kernel,
        out_shape=(half, half),
        grid_spec=pltpu.PrefetchScalarGridSpec(
            num_scalar_prefetch=2,
            grid=(steps,),
            in_specs=[pl.BlockSpec((p.shape[0], INPUT_TILE), lambda k, *_: (0, k)) for p in pieces]
            + [pl.BlockSpec((depth, INPUT_TILE), lambda k, *_: (0, k))],
            out_specs=(whole, whole),
            scratch_shapes=[pltpu.VMEM((tokens, depth), F32)],
        ),
        compiler_params=pltpu.CompilerParams(vmem_limit_bytes=VMEM_LIMIT),
        cost_estimate=pl.CostEstimate(flops=2 * tokens * width * depth, bytes_accessed=16 << 20, transcendentals=0),
    )(keep, slot, *pieces, weight)


def weight_grad(features, slots, pieces, rows):
    width, depth = pieces[0].shape[1], features.shape[2]
    tokens = sum(p.shape[0] for p in pieces)

    def kernel(slot_ref, features_ref, *refs):
        piece_refs, out_ref, sorted_ref = refs[:-2], refs[-2], refs[-1]

        @pl.when(pl.program_id(0) == 0)
        def _():
            at = 0
            for index, (first, last) in enumerate(rows):
                found = features_ref[slot_ref[index]]
                sorted_ref[at : at + last - first] = found[first:last]
                at += last - first

        block = jnp.concatenate([ref[...] for ref in piece_refs], 0)
        out_ref[...] = dot(sorted_ref[...], block, ((0,), (0,))).astype(BF16)

    return pl.pallas_call(
        kernel,
        out_shape=jax.ShapeDtypeStruct((depth, width), BF16),
        grid_spec=pltpu.PrefetchScalarGridSpec(
            num_scalar_prefetch=1,
            grid=(width // WEIGHT_TILE,),
            in_specs=[pl.BlockSpec(features.shape, lambda k, *_: (0, 0, 0))]
            + [pl.BlockSpec((p.shape[0], WEIGHT_TILE), lambda k, *_: (0, k)) for p in pieces],
            out_specs=pl.BlockSpec((depth, WEIGHT_TILE), lambda k, *_: (0, k)),
            scratch_shapes=[pltpu.VMEM((tokens, depth), BF16)],
        ),
        compiler_params=pltpu.CompilerParams(vmem_limit_bytes=VMEM_LIMIT),
        cost_estimate=pl.CostEstimate(flops=2 * depth * tokens * width, bytes_accessed=16 << 20, transcendentals=0),
    )(slots, features, *pieces)


def dot(a, b, dims):
    return lax.dot_general(a, b, (dims, ((), ())), preferred_element_type=F32)


def flat(pieces):
    return [pltpu.with_memory_space_constraint(piece.reshape(-1, piece.shape[-1]), pltpu.HBM) for piece in pieces]


def tie(value, *others):
    return lax.optimization_barrier((value, *others))[0]


def body(inputs, grad_out, weight):
    all_inputs = lax.all_gather(inputs, "col", axis=0, tiled=False)
    place, lane = Place(), Lane()
    cut = lambda k: grad_out[GROUPS[k][0] : GROUPS[k][1]]
    rings, rest = {"b": Ring(lane, cut("late")), "a": Ring(lane, cut("first"))}, []
    for op in ORDER:
        if op == "A":
            rings["f"] = Ring(lane, lane.send(cut("first"), "row", X_FAR))
        elif op == "B":
            rest.append(lane.send(rings["b"].got[len(rest)], "row", X_FAR))
        else:
            rings[op].step()
    pieces = rings["b"].got + rest + rings["a"].got + rings["f"].got
    all_inputs, *pieces = lax.optimization_barrier((all_inputs, *pieces))
    blocks = flat(pieces)
    spans = [GROUPS[k] for k in GROUPS for _ in range(16)]
    mine, other = input_grad_parts(blocks, weight, place, spans)
    mine = mine + lax.ppermute(other, "col", OTHER_CORE)
    total = lax.all_to_all(mine, "col", 0, 0, axis_index_groups=SAME_CORE)
    slots = jnp.stack(2 * place.rows(True))
    out = weight_grad(tie(all_inputs, mine), slots, blocks, spans)
    return out, jnp.sum(total, 0).astype(BF16)


def solution(mesh):
    in_specs = (P("col", "row"), P("row", "col"), P("row", "col"))
    out_specs = (P("row", "col"), P("col", "row"))
    return jax.shard_map(body, mesh=mesh, in_specs=in_specs, out_specs=out_specs, check_vma=False)
```

time: 277 us -> 169 us (0.61)
  waiting for transfers between devices: 233 us -> 70.4 us
  starting transfers between devices: 0.11 us -> 49.6 us
  Pallas kernels: 0 us -> 25.7 us
  matrix products: 25.3 us -> 0 us
  local copies, waits for them, and re-layouts: 0 us -> 3.8 us
  other arithmetic: 1.64 us -> 4.41 us
    all_gather x2 -> x1, waiting for transfers between devices: 175 us -> 0.01 us  [body(): all_inputs = lax.all_gather(inputs, 'col', axis=0, tiled=False)]
    reduce_scatter x1 -> x0, waiting for transfers between devices: 56.7 us -> none  [body(): lax.psum_scatter(partial_value, 'col', scatter_dimension=0, tiled=True)]
    ppermute x0 -> x19, waiting for transfers between devices: none -> 53.1 us  [the longest x18 49 us: send(): out = lax.ppermute(self.after(value), axis, pairs)]
    ppermute x0 -> x19, starting transfers between devices: none -> 45.1 us  [the longest x18 36.8 us: send(): out = lax.ppermute(self.after(value), axis, pairs)]
    pallas_call x0 -> x2, Pallas kernels: none -> 25.7 us  [the longest x1 13.4 us: input_grad_parts(): pl.pallas_call(kernel, out_shape=(half, half), grid_spec=pltpu.PrefetchSc...]
    dot_general x2 -> x0, matrix products: 25.3 us -> none  [the longest x1 13 us: body(): lax.dot_general(all_grads, weight, (((1,), (1,)), ((), ())), preferred_el...]
    all_to_all x0 -> x1, waiting for transfers between devices: none -> 16.6 us  [body(): total = lax.all_to_all(mine, 'col', 0, 0, axis_index_groups=SAME_CORE)]
    all_to_all x0 -> x1, starting transfers between devices: none -> 4.52 us  [body(): total = lax.all_to_all(mine, 'col', 0, 0, axis_index_groups=SAME_CORE)]
  transfers between devices with their start and end apart: 3 -> 21, of which waited for: 3 -> 10; matrix products, arithmetic and copies ran while one was open for 9% -> 1% of each run, Pallas kernels for 0% -> 7%
where the time goes in v1:
time: 169 us; the launch traced here: 168 us
  waiting for transfers between devices  70.4 us (42%)
  starting transfers between devices  49.6 us (29%)
  Pallas kernels  25.7 us (15%)
  between operations  14.3 us (8%)
  other arithmetic  4.41 us (3%)
  local copies, waits for them, and re-layouts  3.8 us (2%)
    ppermute x18, waiting for transfers between devices, send(): out = lax.ppermute(self.after(value), axis, pairs)  49 us
    ppermute x18, starting transfers between devices, send(): out = lax.ppermute(self.after(value), axis, pairs)  36.8 us
    all_to_all x1, waiting for transfers between devices, body(): total = lax.all_to_all(mine, 'col', 0, 0, axis_index_groups=SAME_CORE)  16.6 us
    pallas_call x1, Pallas kernels, input_grad_parts(): pl.pallas_call(kernel, out_shape=(half, half), grid_spec=pltpu.PrefetchSc...  13.4 us
    pallas_call x1, Pallas kernels, weight_grad(): pl.pallas_call(kernel, out_shape=jax.ShapeDtypeStruct((depth, width), BF1...  12.3 us
    ppermute x1, starting transfers between devices, body(): mine = mine + lax.ppermute(other, 'col', OTHER_CORE)  8.28 us
    all_to_all x1, starting transfers between devices, body(): total = lax.all_to_all(mine, 'col', 0, 0, axis_index_groups=SAME_CORE)  4.52 us
    ppermute x1, waiting for transfers between devices, body(): mine = mine + lax.ppermute(other, 'col', OTHER_CORE)  4.16 us
  transfers between devices with their start and end apart: 21, of which 10 were waited for; matrix products, arithmetic and copies ran while one was open for 1% of the time, Pallas kernels for 7%

profile of v1, /device:TPU:1, one launch (start us, length us, event | category | flops | bytes accessed | tf_op | source)
XLA Modules:
  0.0 168.2 jit_solution(670292035620021098)
XLA Ops:
  9.0 3.7 %collective-permute-start.1 = (bf16[48,3072]{1,0:T(8,128)(2,1)S(1)}, bf16[48,3072]{1,0:T(8,128)(2,1)S(1)}, u32[]{:S(2)}, u32[]{:S(2)}) collective-permute-start(bf16[48,3072]{1,0:T(8,128)(2,1)S(1)} %get-tuple-element.79), channel_id=1, source_target_pairs={{0,128},{16,144},{32,160},{48,176},{64,192},{80,208},{96,224},{112... | collective-permute-start | bytes 884744 | tf_op jit(solution)/shard_map/ppermute | solution.py:55
  12.8 5.7 %collective-permute-start = (bf16[1,48,3072]{2,1,0:T(8,128)(2,1)S(1)}, bf16[1,48,3072]{2,1,0:T(8,128)(2,1)S(1)}, u32[]{:S(2)}, u32[]{:S(2)}) collective-permute-start(bf16[1,48,3072]{2,1,0:T(8,128)(2,1)S(1)} %get-tuple-element.55), channel_id=1, source_target_pairs={{0,16},{1,113},{2,18},{3,115},{4,20},{5,117},{6,22},{7,119},{8,24}... | collective-permute-start | bytes 884744 | tf_op jit(solution)/shard_map/ppermute | solution.py:55
  18.5 6.2 %collective-permute-done.5 = bf16[1,48,3072]{2,1,0:T(8,128)(2,1)S(1)} collective-permute-done((bf16[1,48,3072]{2,1,0:T(8,128)(2,1)S(1)}, bf16[1,48,3072]{2,1,0:T(8,128)(2,1)S(1)}, u32[]{:S(2)}, u32[]{:S(2)}) %collective-permute-start.5) | collective-permute-done | bytes 294944 | tf_op jit(solution)/shard_map/ppermute | solution.py:55
  24.7 7.0 %collective-permute-start.14 = (bf16[1,48,3072]{2,1,0:T(8,128)(2,1)S(1)}, bf16[1,48,3072]{2,1,0:T(8,128)(2,1)S(1)}, u32[]{:S(2)}, u32[]{:S(2)}) collective-permute-start(bf16[1,48,3072]{2,1,0:T(8,128)(2,1)S(1)} %bitcast.79), channel_id=1, source_target_pairs={{0,16},{1,113},{2,18},{3,115},{4,20},{5,117},{6,22},{7,119},{8,24}... | collective-permute-start | bytes 884744 | tf_op jit(solution)/shard_map/ppermute | solution.py:55
  31.8 3.7 %collective-permute-start.6 = (bf16[1,48,3072]{2,1,0:T(8,128)(2,1)S(1)}, bf16[1,48,3072]{2,1,0:T(8,128)(2,1)S(1)}, u32[]{:S(2)}, u32[]{:S(2)}) collective-permute-start(bf16[1,48,3072]{2,1,0:T(8,128)(2,1)S(1)} %collective-permute-done), channel_id=1, source_target_pairs={{0,128},{16,144},{32,160},{48,176},{64,192},{80,208},{96,224},{112... | collective-permute-start | bytes 884744 | tf_op jit(solution)/shard_map/ppermute | solution.py:55
  37.4 7.3 %collective-permute-done.2 = bf16[2,48,3072]{2,1,0:T(8,128)(2,1)S(1)} collective-permute-done((bf16[2,48,3072]{2,1,0:T(8,128)(2,1)S(1)}, bf16[2,48,3072]{2,1,0:T(8,128)(2,1)S(1)}, u32[]{:S(2)}, u32[]{:S(2)}) %collective-permute-start.2) | collective-permute-done | bytes 589856 | tf_op jit(solution)/shard_map/ppermute | solution.py:55
  44.7 2.9 %collective-permute-start.3 = (bf16[2,48,3072]{2,1,0:T(8,128)(2,1)S(1)}, bf16[2,48,3072]{2,1,0:T(8,128)(2,1)S(1)}, u32[]{:S(2)}, u32[]{:S(2)}) collective-permute-start(bf16[2,48,3072]{2,1,0:T(8,128)(2,1)S(1)} %collective-permute-done.2), channel_id=1, source_target_pairs={{0,16},{1,113},{2,18},{3,115},{4,20},{5,117},{6,22},{7,119},{8,24}... | collective-permute-start | bytes 1769480 | tf_op jit(solution)/shard_map/ppermute | solution.py:55
  47.6 2.2 %collective-permute-start.7 = (bf16[2,48,3072]{2,1,0:T(8,128)(2,1)S(1)}, bf16[2,48,3072]{2,1,0:T(8,128)(2,1)S(1)}, u32[]{:S(2)}, u32[]{:S(2)}) collective-permute-start(bf16[2,48,3072]{2,1,0:T(8,128)(2,1)S(1)} %collective-permute-done.2), channel_id=1, source_target_pairs={{0,128},{16,144},{32,160},{48,176},{64,192},{80,208},{96,224},{112... | collective-permute-start | bytes 1769480 | tf_op jit(solution)/shard_map/ppermute | solution.py:55
  51.1 3.0 %collective-permute-start.12 = (bf16[2,48,3072]{2,1,0:T(8,128)(2,1)S(1)}, bf16[2,48,3072]{2,1,0:T(8,128)(2,1)}, u32[]{:S(2)}, u32[]{:S(2)}) collective-permute-start(bf16[2,48,3072]{2,1,0:T(8,128)(2,1)S(1)} %collective-permute-done.11), channel_id=1, source_target_pairs={{0,16},{1,113},{2,18},{3,115},{4,20},{5,117},{6,22},{7,119},{8,24}... | collective-permute-start | bytes 1769480 | tf_op jit(solution)/shard_map/ppermute | solution.py:55
  54.0 9.4 %collective-permute-done.15 = bf16[2,48,3072]{2,1,0:T(8,128)(2,1)S(1)} collective-permute-done((bf16[2,48,3072]{2,1,0:T(8,128)(2,1)S(1)}, bf16[2,48,3072]{2,1,0:T(8,128)(2,1)S(1)}, u32[]{:S(2)}, u32[]{:S(2)}) %collective-permute-start.15) | collective-permute-done | bytes 589856 | tf_op jit(solution)/shard_map/ppermute | solution.py:55
  63.5 3.0 %collective-permute-start.16 = (bf16[2,48,3072]{2,1,0:T(8,128)(2,1)S(1)}, bf16[2,48,3072]{2,1,0:T(8,128)(2,1)}, u32[]{:S(2)}, u32[]{:S(2)}) collective-permute-start(bf16[2,48,3072]{2,1,0:T(8,128)(2,1)S(1)} %collective-permute-done.15), channel_id=1, source_target_pairs={{0,16},{1,113},{2,18},{3,115},{4,20},{5,117},{6,22},{7,119},{8,24}... | collective-permute-start | bytes 1769480 | tf_op jit(solution)/shard_map/ppermute | solution.py:55
  66.5 2.4 %collective-permute-start.8 = (bf16[2,48,3072]{2,1,0:T(8,128)(2,1)S(1)}, bf16[2,48,3072]{2,1,0:T(8,128)(2,1)S(1)}, u32[]{:S(2)}, u32[]{:S(2)}) collective-permute-start(bf16[2,48,3072]{2,1,0:T(8,128)(2,1)S(1)} %collective-permute-done.3), channel_id=1, source_target_pairs={{0,128},{16,144},{32,160},{48,176},{64,192},{80,208},{96,224},{112... | collective-permute-start | bytes 1769480 | tf_op jit(solution)/shard_map/ppermute | solution.py:55
  68.9 3.6 %collective-permute-done.12 = bf16[2,48,3072]{2,1,0:T(8,128)(2,1)} collective-permute-done((bf16[2,48,3072]{2,1,0:T(8,128)(2,1)S(1)}, bf16[2,48,3072]{2,1,0:T(8,128)(2,1)}, u32[]{:S(2)}, u32[]{:S(2)}) %collective-permute-start.12) | collective-permute-done | bytes 589856 | tf_op jit(solution)/shard_map/ppermute | solution.py:55
  72.5 8.4 %collective-permute-done.16 = bf16[2,48,3072]{2,1,0:T(8,128)(2,1)} collective-permute-done((bf16[2,48,3072]{2,1,0:T(8,128)(2,1)S(1)}, bf16[2,48,3072]{2,1,0:T(8,128)(2,1)}, u32[]{:S(2)}, u32[]{:S(2)}) %collective-permute-start.16) | collective-permute-done | bytes 589856 | tf_op jit(solution)/shard_map/ppermute | solution.py:55
  82.5 6.5 %collective-permute-done.13 = bf16[2,48,3072]{2,1,0:T(8,128)(2,1)} collective-permute-done((bf16[2,48,3072]{2,1,0:T(8,128)(2,1)}, bf16[2,48,3072]{2,1,0:T(8,128)(2,1)}, u32[]{:S(2)}, u32[]{:S(2)}) %collective-permute-start.13) | collective-permute-done | bytes 589856 | tf_op jit(solution)/shard_map/ppermute | solution.py:55
  89.0 6.3 %collective-permute-done.17 = bf16[2,48,3072]{2,1,0:T(8,128)(2,1)} collective-permute-done((bf16[2,48,3072]{2,1,0:T(8,128)(2,1)}, bf16[2,48,3072]{2,1,0:T(8,128)(2,1)}, u32[]{:S(2)}, u32[]{:S(2)}) %collective-permute-start.17) | collective-permute-done | bytes 589856 | tf_op jit(solution)/shard_map/ppermute | solution.py:55
  95.4 2.3 %copy-done = bf16[768,3072]{1,0:T(8,128)(2,1)S(1)} copy-done((bf16[768,3072]{1,0:T(8,128)(2,1)S(1)}, bf16[768,3072]{1,0:T(8,128)(2,1)}, u32[]{:S(2)}) %copy-start) | copy-done | bytes 4718616
  97.7 13.4 %shard_map.50 = (f32[8,96,768]{2,1,0:T(8,128)S(1)}, f32[8,96,768]{2,1,0:T(8,128)S(1)}) custom-call(s32[16]{0:T(128)S(1)} %stack.202.keep_ref, s32[16]{0:T(128)S(1)} %stack.219.slot_ref, bf16[48,3072]{1,0:T(8,128)(2,1)} %bitcast.77, bf16[48,3072]{1,0:T(8,128)(2,1)} %bitcast.81, bf16[96,3072]{1,0:T(8,128)(2,1)} %bitcast.87, bf16[96,3072]{1,0:T(8,128)(2,1)} %bitcast.93, ...), custom_call_target="tpu_custom_call" | custom-call | flops 7247757312 | bytes 16777216 | tf_op jit(solution)/shard_map/pallas_call | solution.py:121
  111.1 8.3 %collective-permute-start.18 = (f32[8,96,768]{2,1,0:T(8,128)S(1)}, f32[8,96,768]{2,1,0:T(8,128)S(1)}, u32[]{:S(2)}, u32[]{:S(2)}) collective-permute-start(f32[8,96,768]{2,1,0:T(8,128)S(1)} %get-tuple-element.76), channel_id=1, source_target_pairs={{0,1},{1,0},{2,3},{3,2},{4,5},{5,4},{6,7},{7,6},{8,9},{9,8},{10,11... | collective-permute-start | bytes 7077896 | tf_op jit(solution)/shard_map/ppermute | solution.py:200
  119.4 4.2 %collective-permute-done.18 = f32[8,96,768]{2,1,0:T(8,128)S(1)} collective-permute-done((f32[8,96,768]{2,1,0:T(8,128)S(1)}, f32[8,96,768]{2,1,0:T(8,128)S(1)}, u32[]{:S(2)}, u32[]{:S(2)}) %collective-permute-start.18) | collective-permute-done | bytes 2359328 | tf_op jit(solution)/shard_map/ppermute | solution.py:200
  125.3 4.5 %all-to-all-start = ((f32[8,96,768]{2,1,0:T(8,128)}), f32[8,96,768]{2,1,0:T(8,128)}, u32[]{:S(2)}, u32[]{:S(2)}) async-start(f32[8,96,768]{2,1,0:T(8,128)} %add.399), calls=%async_computation | async-start | bytes 4718592 | tf_op jit(solution)/shard_map/all_to_all | solution.py:201
  130.0 12.3 %shard_map.51 = bf16[768,3072]{1,0:T(8,128)(2,1)} custom-call(s32[32]{0:T(128)S(1)} %stack.185.slot_ref, bf16[16,96,768]{2,1,0:T(8,128)(2,1)S(1)} %bitcast.74, bf16[48,3072]{1,0:T(8,128)(2,1)} %bitcast.78, bf16[48,3072]{1,0:T(8,128)(2,1)} %bitcast.82, bf16[96,3072]{1,0:T(8,128)(2,1)} %bitcast.88, bf16[96,3072]{1,0:T(8,128)(2,1)} %bitcast.94, ...), custom_call_target="tpu_custom_call" | custom-call | flops 7247757312 | bytes 16777216 | tf_op jit(solution)/shard_map/pallas_call | solution.py:155
  142.3 16.6 %all-to-all-done = f32[8,96,768]{2,1,0:T(8,128)} async-done(((f32[8,96,768]{2,1,0:T(8,128)}), f32[8,96,768]{2,1,0:T(8,128)}, u32[]{:S(2)}, u32[]{:S(2)}) %all-to-all-start) | async-done | bytes 2359328 | tf_op jit(solution)/shard_map/all_to_all | solution.py:201
  158.9 2.5 %reduce_sum.9 = bf16[96,768]{1,0:T(8,128)(2,1)} reduce(f32[8,96,768]{2,1,0:T(8,128)} %all-to-all-done, f32[]{:T(128)} %constant.382.clone.1), dimensions={0}, to_apply=%region_0.1 | reduce | flops 516096 | bytes 2506756 | tf_op jit(solution)/shard_map/reduce_sum | solution.py:204
  (62 shorter events, 8.6 us)
Async XLA Ops:
  7.2 88.1 %all-gather.3.cloned.1.call-start = ((), (), s32[]{:S(2)}) async-start(), calls=%async_computation.1 | async-start | bytes 2506752 | tf_op jit(solution)/shard_map/all_gather | solution.py:184
  9.0 86.3 %copy-start.2 = (bf16[1,48,3072]{2,1,0:T(8,128)(2,1)}, bf16[1,48,3072]{2,1,0:T(8,128)(2,1)S(1)}, u32[]{:S(2)}) copy-start(bf16[1,48,3072]{2,1,0:T(8,128)(2,1)S(1)} %get-tuple-element.65) | copy-start | bytes 884740
  9.0 86.3 %copy-start.3 = (bf16[1,48,3072]{2,1,0:T(8,128)(2,1)}, bf16[1,48,3072]{2,1,0:T(8,128)(2,1)S(1)}, u32[]{:S(2)}) copy-start(bf16[1,48,3072]{2,1,0:T(8,128)(2,1)S(1)} %get-tuple-element.55) | copy-start | bytes 884740
  9.0 9.5 %collective-permute-start.1 = (bf16[48,3072]{1,0:T(8,128)(2,1)S(1)}, bf16[48,3072]{1,0:T(8,128)(2,1)S(1)}, u32[]{:S(2)}, u32[]{:S(2)}) collective-permute-start(bf16[48,3072]{1,0:T(8,128)(2,1)S(1)} %get-tuple-element.79), channel_id=1, source_target_pairs={{0,128},{16,144},{32,160},{48,176},{64,192},{80,208},{96,224},{112... | collective-permute-start | bytes 884744 | tf_op jit(solution)/shard_map/ppermute | solution.py:55
  12.7 12.0 %collective-permute-start.5 = (bf16[1,48,3072]{2,1,0:T(8,128)(2,1)S(1)}, bf16[1,48,3072]{2,1,0:T(8,128)(2,1)S(1)}, u32[]{:S(2)}, u32[]{:S(2)}) collective-permute-start(bf16[1,48,3072]{2,1,0:T(8,128)(2,1)S(1)} %get-tuple-element.55), channel_id=1, source_target_pairs={{0,128},{16,144},{32,160},{48,176},{64,192},{80,208},{96,224},{112... | collective-permute-start | bytes 884744 | tf_op jit(solution)/shard_map/ppermute | solution.py:55
  12.8 18.9 %collective-permute-start = (bf16[1,48,3072]{2,1,0:T(8,128)(2,1)S(1)}, bf16[1,48,3072]{2,1,0:T(8,128)(2,1)S(1)}, u32[]{:S(2)}, u32[]{:S(2)}) collective-permute-start(bf16[1,48,3072]{2,1,0:T(8,128)(2,1)S(1)} %get-tuple-element.55), channel_id=1, source_target_pairs={{0,16},{1,113},{2,18},{3,115},{4,20},{5,117},{6,22},{7,119},{8,24}... | collective-permute-start | bytes 884744 | tf_op jit(solution)/shard_map/ppermute | solution.py:55
  18.5 17.1 %collective-permute-start.10 = (bf16[1,48,3072]{2,1,0:T(8,128)(2,1)S(1)}, bf16[1,48,3072]{2,1,0:T(8,128)(2,1)S(1)}, u32[]{:S(2)}, u32[]{:S(2)}) collective-permute-start(bf16[1,48,3072]{2,1,0:T(8,128)(2,1)S(1)} %get-tuple-element.65), channel_id=1, source_target_pairs={{0,16},{1,113},{2,18},{3,115},{4,20},{5,117},{6,22},{7,119},{8,24}... | collective-permute-start | bytes 884744 | tf_op jit(solution)/shard_map/ppermute | solution.py:55
  18.5 76.8 %copy-start.4 = (bf16[48,3072]{1,0:T(8,128)(2,1)}, bf16[48,3072]{1,0:T(8,128)(2,1)S(1)}, u32[]{:S(2)}) copy-start(bf16[48,3072]{1,0:T(8,128)(2,1)S(1)} %collective-permute-done.1) | copy-start | bytes 884740
  24.7 12.5 %collective-permute-start.14 = (bf16[1,48,3072]{2,1,0:T(8,128)(2,1)S(1)}, bf16[1,48,3072]{2,1,0:T(8,128)(2,1)S(1)}, u32[]{:S(2)}, u32[]{:S(2)}) collective-permute-start(bf16[1,48,3072]{2,1,0:T(8,128)(2,1)S(1)} %bitcast.79), channel_id=1, source_target_pairs={{0,16},{1,113},{2,18},{3,115},{4,20},{5,117},{6,22},{7,119},{8,24}... | collective-permute-start | bytes 884744 | tf_op jit(solution)/shard_map/ppermute | solution.py:55
  31.8 15.8 %collective-permute-start.6 = (bf16[1,48,3072]{2,1,0:T(8,128)(2,1)S(1)}, bf16[1,48,3072]{2,1,0:T(8,128)(2,1)S(1)}, u32[]{:S(2)}, u32[]{:S(2)}) collective-permute-start(bf16[1,48,3072]{2,1,0:T(8,128)(2,1)S(1)} %collective-permute-done), channel_id=1, source_target_pairs={{0,128},{16,144},{32,160},{48,176},{64,192},{80,208},{96,224},{112... | collective-permute-start | bytes 884744 | tf_op jit(solution)/shard_map/ppermute | solution.py:55
  35.5 9.2 %collective-permute-start.2 = (bf16[2,48,3072]{2,1,0:T(8,128)(2,1)S(1)}, bf16[2,48,3072]{2,1,0:T(8,128)(2,1)S(1)}, u32[]{:S(2)}, u32[]{:S(2)}) collective-permute-start(bf16[2,48,3072]{2,1,0:T(8,128)(2,1)S(1)} %pad_maximum_fusion), channel_id=1, source_target_pairs={{0,112},{1,17},{2,114},{3,19},{4,116},{5,21},{6,118},{7,23},{8,120... | collective-permute-start | bytes 1769480 | tf_op jit(solution)/shard_map/ppermute | solution.py:55
  35.7 15.4 %collective-permute-start.11 = (bf16[2,48,3072]{2,1,0:T(8,128)(2,1)S(1)}, bf16[2,48,3072]{2,1,0:T(8,128)(2,1)S(1)}, u32[]{:S(2)}, u32[]{:S(2)}) collective-permute-start(bf16[2,48,3072]{2,1,0:T(8,128)(2,1)S(1)} %pad_maximum_fusion.1), channel_id=1, source_target_pairs={{0,112},{1,17},{2,114},{3,19},{4,116},{5,21},{6,118},{7,23},{8,120... | collective-permute-start | bytes 1769480 | tf_op jit(solution)/shard_map/ppermute | solution.py:55
  37.3 26.2 %collective-permute-start.15 = (bf16[2,48,3072]{2,1,0:T(8,128)(2,1)S(1)}, bf16[2,48,3072]{2,1,0:T(8,128)(2,1)S(1)}, u32[]{:S(2)}, u32[]{:S(2)}) collective-permute-start(bf16[2,48,3072]{2,1,0:T(8,128)(2,1)S(1)} %pad_maximum_fusion.2), channel_id=1, source_target_pairs={{0,112},{1,17},{2,114},{3,19},{4,116},{5,21},{6,118},{7,23},{8,120... | collective-permute-start | bytes 1769480 | tf_op jit(solution)/shard_map/ppermute | solution.py:55
  44.7 21.7 %collective-permute-start.3 = (bf16[2,48,3072]{2,1,0:T(8,128)(2,1)S(1)}, bf16[2,48,3072]{2,1,0:T(8,128)(2,1)S(1)}, u32[]{:S(2)}, u32[]{:S(2)}) collective-permute-start(bf16[2,48,3072]{2,1,0:T(8,128)(2,1)S(1)} %collective-permute-done.2), channel_id=1, source_target_pairs={{0,16},{1,113},{2,18},{3,115},{4,20},{5,117},{6,22},{7,119},{8,24}... | collective-permute-start | bytes 1769480 | tf_op jit(solution)/shard_map/ppermute | solution.py:55
  47.6 18.9 %collective-permute-start.7 = (bf16[2,48,3072]{2,1,0:T(8,128)(2,1)S(1)}, bf16[2,48,3072]{2,1,0:T(8,128)(2,1)S(1)}, u32[]{:S(2)}, u32[]{:S(2)}) collective-permute-start(bf16[2,48,3072]{2,1,0:T(8,128)(2,1)S(1)} %collective-permute-done.2), channel_id=1, source_target_pairs={{0,128},{16,144},{32,160},{48,176},{64,192},{80,208},{96,224},{112... | collective-permute-start | bytes 1769480 | tf_op jit(solution)/shard_map/ppermute | solution.py:55
  51.1 21.5 %collective-permute-start.12 = (bf16[2,48,3072]{2,1,0:T(8,128)(2,1)S(1)}, bf16[2,48,3072]{2,1,0:T(8,128)(2,1)}, u32[]{:S(2)}, u32[]{:S(2)}) collective-permute-start(bf16[2,48,3072]{2,1,0:T(8,128)(2,1)S(1)} %collective-permute-done.11), channel_id=1, source_target_pairs={{0,16},{1,113},{2,18},{3,115},{4,20},{5,117},{6,22},{7,119},{8,24}... | collective-permute-start | bytes 1769480 | tf_op jit(solution)/shard_map/ppermute | solution.py:55
  63.5 17.4 %collective-permute-start.16 = (bf16[2,48,3072]{2,1,0:T(8,128)(2,1)S(1)}, bf16[2,48,3072]{2,1,0:T(8,128)(2,1)}, u32[]{:S(2)}, u32[]{:S(2)}) collective-permute-start(bf16[2,48,3072]{2,1,0:T(8,128)(2,1)S(1)} %collective-permute-done.15), channel_id=1, source_target_pairs={{0,16},{1,113},{2,18},{3,115},{4,20},{5,117},{6,22},{7,119},{8,24}... | collective-permute-start | bytes 1769480 | tf_op jit(solution)/shard_map/ppermute | solution.py:55
  66.4 14.5 %collective-permute-start.4 = (bf16[2,48,3072]{2,1,0:T(8,128)(2,1)S(1)}, bf16[2,48,3072]{2,1,0:T(8,128)(2,1)}, u32[]{:S(2)}, u32[]{:S(2)}) collective-permute-start(bf16[2,48,3072]{2,1,0:T(8,128)(2,1)S(1)} %collective-permute-done.3), channel_id=1, source_target_pairs={{0,112},{1,17},{2,114},{3,19},{4,116},{5,21},{6,118},{7,23},{8,120... | collective-permute-start | bytes 1769480 | tf_op jit(solution)/shard_map/ppermute | solution.py:55
  66.5 14.5 %collective-permute-start.8 = (bf16[2,48,3072]{2,1,0:T(8,128)(2,1)S(1)}, bf16[2,48,3072]{2,1,0:T(8,128)(2,1)S(1)}, u32[]{:S(2)}, u32[]{:S(2)}) collective-permute-start(bf16[2,48,3072]{2,1,0:T(8,128)(2,1)S(1)} %collective-permute-done.3), channel_id=1, source_target_pairs={{0,128},{16,144},{32,160},{48,176},{64,192},{80,208},{96,224},{112... | collective-permute-start | bytes 1769480 | tf_op jit(solution)/shard_map/ppermute | solution.py:55
  72.5 16.4 %collective-permute-start.13 = (bf16[2,48,3072]{2,1,0:T(8,128)(2,1)}, bf16[2,48,3072]{2,1,0:T(8,128)(2,1)}, u32[]{:S(2)}, u32[]{:S(2)}) collective-permute-start(bf16[2,48,3072]{2,1,0:T(8,128)(2,1)} %collective-permute-done.12), channel_id=1, source_target_pairs={{0,112},{1,17},{2,114},{3,19},{4,116},{5,21},{6,118},{7,23},{8,120... | collective-permute-start | bytes 1769480 | tf_op jit(solution)/shard_map/ppermute | solution.py:55
  80.9 14.4 %collective-permute-start.17 = (bf16[2,48,3072]{2,1,0:T(8,128)(2,1)}, bf16[2,48,3072]{2,1,0:T(8,128)(2,1)}, u32[]{:S(2)}, u32[]{:S(2)}) collective-permute-start(bf16[2,48,3072]{2,1,0:T(8,128)(2,1)} %collective-permute-done.16), channel_id=1, source_target_pairs={{0,112},{1,17},{2,114},{3,19},{4,116},{5,21},{6,118},{7,23},{8,120... | collective-permute-start | bytes 1769480 | tf_op jit(solution)/shard_map/ppermute | solution.py:55
  81.0 14.3 %collective-permute-start.9 = (bf16[2,48,3072]{2,1,0:T(8,128)(2,1)}, bf16[2,48,3072]{2,1,0:T(8,128)(2,1)}, u32[]{:S(2)}, u32[]{:S(2)}) collective-permute-start(bf16[2,48,3072]{2,1,0:T(8,128)(2,1)} %collective-permute-done.4), channel_id=1, source_target_pairs={{0,128},{16,144},{32,160},{48,176},{64,192},{80,208},{96,224},{112... | collective-permute-start | bytes 1769480 | tf_op jit(solution)/shard_map/ppermute | solution.py:55
  111.1 12.4 %collective-permute-start.18 = (f32[8,96,768]{2,1,0:T(8,128)S(1)}, f32[8,96,768]{2,1,0:T(8,128)S(1)}, u32[]{:S(2)}, u32[]{:S(2)}) collective-permute-start(f32[8,96,768]{2,1,0:T(8,128)S(1)} %get-tuple-element.76), channel_id=1, source_target_pairs={{0,1},{1,0},{2,3},{3,2},{4,5},{5,4},{6,7},{7,6},{8,9},{9,8},{10,11... | collective-permute-start | bytes 7077896 | tf_op jit(solution)/shard_map/ppermute | solution.py:200
  125.3 33.6 %all-to-all-start = ((f32[8,96,768]{2,1,0:T(8,128)}), f32[8,96,768]{2,1,0:T(8,128)}, u32[]{:S(2)}, u32[]{:S(2)}) async-start(f32[8,96,768]{2,1,0:T(8,128)} %add.399), calls=%async_computation | async-start | bytes 4718592 | tf_op jit(solution)/shard_map/all_to_all | solution.py:201
  (13 other events, 428.1 us)
Sparse Core Ops, SparseCore 0:
  9.8 42.7 all-gather.2

commit v2 on v1

--- a/solution.py
+++ b/solution.py
@@ -131,7 +131,7 @@
         ),
         compiler_params=pltpu.CompilerParams(vmem_limit_bytes=VMEM_LIMIT),
         cost_estimate=pl.CostEstimate(flops=2 * tokens * width * depth, bytes_accessed=16 << 20, transcendentals=0),
-    )(keep, slot, *pieces, weight)
+    )(keep, slot, *pieces, pltpu.with_memory_space_constraint(weight, pltpu.HBM))
 
 
 def weight_grad(features, slots, pieces, rows):
@@ -193,7 +193,7 @@
         else:
             rings[op].step()
     pieces = rings["b"].got + rest + rings["a"].got + rings["f"].got
-    all_inputs, *pieces = lax.optimization_barrier((all_inputs, *pieces))
+    pieces = lax.optimization_barrier(pieces)
     blocks = flat(pieces)
     spans = [GROUPS[k] for k in GROUPS for _ in range(16)]
     mine, other = input_grad_parts(blocks, weight, place, spans)

time: 169 us -> 158 us (0.935)
  starting transfers between devices: 49.6 us -> 38.6 us
  other arithmetic: 4.41 us -> 2.72 us
    ppermute x18, starting transfers between devices: 36.8 us -> 29.8 us  [send(): out = lax.ppermute(self.after(value), axis, pairs)]
    ppermute x1, starting transfers between devices: 8.28 us -> 3.98 us  [body(): mine = mine + lax.ppermute(other, 'col', OTHER_CORE)]
    all_to_all x1, waiting for transfers between devices: 16.6 us -> 13.7 us  [body(): total = lax.all_to_all(mine, 'col', 0, 0, axis_index_groups=SAME_CORE)]
    ppermute x18, waiting for transfers between devices: 49 us -> 51.6 us  [send(): out = lax.ppermute(self.after(value), axis, pairs)]
  transfers between devices with their start and end apart: 21 -> 21, of which waited for: 10 -> 16; matrix products, arithmetic and copies ran while one was open for 1% -> 1% of each run, Pallas kernels for 7% -> 17%
where the time goes in v2:
time: 158 us; the launch traced here: 157 us
  waiting for transfers between devices  70.9 us (45%)
  starting transfers between devices  38.6 us (24%)
  Pallas kernels  25.9 us (16%)
  between operations  15.2 us (10%)
  local copies, waits for them, and re-layouts  3.88 us (2%)
  other arithmetic  2.72 us (2%)
    ppermute x18, waiting for transfers between devices, send(): out = lax.ppermute(self.after(value), axis, pairs)  51.6 us
    ppermute x18, starting transfers between devices, send(): out = lax.ppermute(self.after(value), axis, pairs)  29.8 us
    all_to_all x1, waiting for transfers between devices, body(): total = lax.all_to_all(mine, 'col', 0, 0, axis_index_groups=SAME_CORE)  13.7 us
    pallas_call x1, Pallas kernels, input_grad_parts(): pl.pallas_call(kernel, out_shape=(half, half), grid_spec=pltpu.PrefetchSc...  13.7 us
    pallas_call x1, Pallas kernels, weight_grad(): pl.pallas_call(kernel, out_shape=jax.ShapeDtypeStruct((depth, width), BF1...  12.3 us
    all_to_all x1, starting transfers between devices, body(): total = lax.all_to_all(mine, 'col', 0, 0, axis_index_groups=SAME_CORE)  4.71 us
    ppermute x1, waiting for transfers between devices, body(): mine = mine + lax.ppermute(other, 'col', OTHER_CORE)  4.32 us
    ppermute x1, starting transfers between devices, body(): mine = mine + lax.ppermute(other, 'col', OTHER_CORE)  3.98 us
  transfers between devices with their start and end apart: 21, of which 16 were waited for; matrix products, arithmetic and copies ran while one was open for 1% of the time, Pallas kernels for 17%

profile of v2, /device:TPU:1, one launch (start us, length us, event | category | flops | bytes accessed | tf_op | source)
XLA Modules:
  0.0 157.1 jit_solution(18018051466754704485)
XLA Ops:
  8.4 6.5 %collective-permute-start = (bf16[1,48,3072]{2,1,0:T(8,128)(2,1)S(1)}, bf16[1,48,3072]{2,1,0:T(8,128)(2,1)S(1)}, u32[]{:S(2)}, u32[]{:S(2)}) collective-permute-start(bf16[1,48,3072]{2,1,0:T(8,128)(2,1)S(1)} %get-tuple-element.53), channel_id=1, source_target_pairs={{0,16},{1,113},{2,18},{3,115},{4,20},{5,117},{6,22},{7,119},{8,24}... | collective-permute-start | bytes 884744 | tf_op jit(solution)/shard_map/ppermute | solution.py:55
  14.8 2.7 %collective-permute-start.5 = (bf16[1,48,3072]{2,1,0:T(8,128)(2,1)S(1)}, bf16[1,48,3072]{2,1,0:T(8,128)(2,1)S(1)}, u32[]{:S(2)}, u32[]{:S(2)}) collective-permute-start(bf16[1,48,3072]{2,1,0:T(8,128)(2,1)S(1)} %get-tuple-element.53), channel_id=1, source_target_pairs={{0,128},{16,144},{32,160},{48,176},{64,192},{80,208},{96,224},{112... | collective-permute-start | bytes 884744 | tf_op jit(solution)/shard_map/ppermute | solution.py:55
  19.3 9.6 %collective-permute-done.1 = bf16[48,3072]{1,0:T(8,128)(2,1)S(1)} collective-permute-done((bf16[48,3072]{1,0:T(8,128)(2,1)S(1)}, bf16[48,3072]{1,0:T(8,128)(2,1)S(1)}, u32[]{:S(2)}, u32[]{:S(2)}) %collective-permute-start.1) | collective-permute-done | bytes 294944 | tf_op jit(solution)/shard_map/ppermute | solution.py:55
  28.9 2.7 %collective-permute-start.6 = (bf16[1,48,3072]{2,1,0:T(8,128)(2,1)S(1)}, bf16[1,48,3072]{2,1,0:T(8,128)(2,1)S(1)}, u32[]{:S(2)}, u32[]{:S(2)}) collective-permute-start(bf16[1,48,3072]{2,1,0:T(8,128)(2,1)S(1)} %collective-permute-done), channel_id=1, source_target_pairs={{0,128},{16,144},{32,160},{48,176},{64,192},{80,208},{96,224},{112... | collective-permute-start | bytes 884744 | tf_op jit(solution)/shard_map/ppermute | solution.py:55
  31.6 2.8 %collective-permute-start.14 = (bf16[1,48,3072]{2,1,0:T(8,128)(2,1)S(1)}, bf16[1,48,3072]{2,1,0:T(8,128)(2,1)S(1)}, u32[]{:S(2)}, u32[]{:S(2)}) collective-permute-start(bf16[1,48,3072]{2,1,0:T(8,128)(2,1)S(1)} %bitcast.81), channel_id=1, source_target_pairs={{0,16},{1,113},{2,18},{3,115},{4,20},{5,117},{6,22},{7,119},{8,24}... | collective-permute-start | bytes 884744 | tf_op jit(solution)/shard_map/ppermute | solution.py:55
  37.9 4.4 %collective-permute-start.7 = (bf16[2,48,3072]{2,1,0:T(8,128)(2,1)S(1)}, bf16[2,48,3072]{2,1,0:T(8,128)(2,1)S(1)}, u32[]{:S(2)}, u32[]{:S(2)}) collective-permute-start(bf16[2,48,3072]{2,1,0:T(8,128)(2,1)S(1)} %collective-permute-done.2), channel_id=1, source_target_pairs={{0,128},{16,144},{32,160},{48,176},{64,192},{80,208},{96,224},{112... | collective-permute-start | bytes 1769480 | tf_op jit(solution)/shard_map/ppermute | solution.py:55
  42.3 2.4 %collective-permute-start.3 = (bf16[2,48,3072]{2,1,0:T(8,128)(2,1)S(1)}, bf16[2,48,3072]{2,1,0:T(8,128)(2,1)S(1)}, u32[]{:S(2)}, u32[]{:S(2)}) collective-permute-start(bf16[2,48,3072]{2,1,0:T(8,128)(2,1)S(1)} %collective-permute-done.2), channel_id=1, source_target_pairs={{0,16},{1,113},{2,18},{3,115},{4,20},{5,117},{6,22},{7,119},{8,24}... | collective-permute-start | bytes 1769480 | tf_op jit(solution)/shard_map/ppermute | solution.py:55
  45.3 2.1 %collective-permute-done.11 = bf16[2,48,3072]{2,1,0:T(8,128)(2,1)S(1)} collective-permute-done((bf16[2,48,3072]{2,1,0:T(8,128)(2,1)S(1)}, bf16[2,48,3072]{2,1,0:T(8,128)(2,1)S(1)}, u32[]{:S(2)}, u32[]{:S(2)}) %collective-permute-start.11) | collective-permute-done | bytes 589856 | tf_op jit(solution)/shard_map/ppermute | solution.py:55
  48.7 2.9 %collective-permute-done.7 = bf16[2,48,3072]{2,1,0:T(8,128)(2,1)S(1)} collective-permute-done((bf16[2,48,3072]{2,1,0:T(8,128)(2,1)S(1)}, bf16[2,48,3072]{2,1,0:T(8,128)(2,1)S(1)}, u32[]{:S(2)}, u32[]{:S(2)}) %collective-permute-start.7) | collective-permute-done | bytes 589856 | tf_op jit(solution)/shard_map/ppermute | solution.py:55
  51.6 7.4 %collective-permute-done.3 = bf16[2,48,3072]{2,1,0:T(8,128)(2,1)S(1)} collective-permute-done((bf16[2,48,3072]{2,1,0:T(8,128)(2,1)S(1)}, bf16[2,48,3072]{2,1,0:T(8,128)(2,1)S(1)}, u32[]{:S(2)}, u32[]{:S(2)}) %collective-permute-start.3) | collective-permute-done | bytes 589856 | tf_op jit(solution)/shard_map/ppermute | solution.py:55
  61.7 8.4 %collective-permute-done.12 = bf16[2,48,3072]{2,1,0:T(8,128)(2,1)} collective-permute-done((bf16[2,48,3072]{2,1,0:T(8,128)(2,1)S(1)}, bf16[2,48,3072]{2,1,0:T(8,128)(2,1)}, u32[]{:S(2)}, u32[]{:S(2)}) %collective-permute-start.12) | collective-permute-done | bytes 589856 | tf_op jit(solution)/shard_map/ppermute | solution.py:55
  70.0 3.6 %collective-permute-done.8 = bf16[2,48,3072]{2,1,0:T(8,128)(2,1)S(1)} collective-permute-done((bf16[2,48,3072]{2,1,0:T(8,128)(2,1)S(1)}, bf16[2,48,3072]{2,1,0:T(8,128)(2,1)S(1)}, u32[]{:S(2)}, u32[]{:S(2)}) %collective-permute-start.8) | collective-permute-done | bytes 589856 | tf_op jit(solution)/shard_map/ppermute | solution.py:55
  74.5 3.0 %collective-permute-start.9 = (bf16[2,48,3072]{2,1,0:T(8,128)(2,1)}, bf16[2,48,3072]{2,1,0:T(8,128)(2,1)}, u32[]{:S(2)}, u32[]{:S(2)}) collective-permute-start(bf16[2,48,3072]{2,1,0:T(8,128)(2,1)} %collective-permute-done.4), channel_id=1, source_target_pairs={{0,128},{16,144},{32,160},{48,176},{64,192},{80,208},{96,224},{112... | collective-permute-start | bytes 1769480 | tf_op jit(solution)/shard_map/ppermute | solution.py:55
  77.5 5.2 %collective-permute-done.16 = bf16[2,48,3072]{2,1,0:T(8,128)(2,1)} collective-permute-done((bf16[2,48,3072]{2,1,0:T(8,128)(2,1)S(1)}, bf16[2,48,3072]{2,1,0:T(8,128)(2,1)}, u32[]{:S(2)}, u32[]{:S(2)}) %collective-permute-start.16) | collective-permute-done | bytes 589856 | tf_op jit(solution)/shard_map/ppermute | solution.py:55
  83.9 1.7 %collective-permute-done.13 = bf16[2,48,3072]{2,1,0:T(8,128)(2,1)} collective-permute-done((bf16[2,48,3072]{2,1,0:T(8,128)(2,1)}, bf16[2,48,3072]{2,1,0:T(8,128)(2,1)}, u32[]{:S(2)}, u32[]{:S(2)}) %collective-permute-start.13) | collective-permute-done | bytes 589856 | tf_op jit(solution)/shard_map/ppermute | solution.py:55
  85.6 6.4 %collective-permute-done.17 = bf16[2,48,3072]{2,1,0:T(8,128)(2,1)} collective-permute-done((bf16[2,48,3072]{2,1,0:T(8,128)(2,1)}, bf16[2,48,3072]{2,1,0:T(8,128)(2,1)}, u32[]{:S(2)}, u32[]{:S(2)}) %collective-permute-start.17) | collective-permute-done | bytes 589856 | tf_op jit(solution)/shard_map/ppermute | solution.py:55
  92.1 13.7 %shard_map.50 = (f32[8,96,768]{2,1,0:T(8,128)S(1)}, f32[8,96,768]{2,1,0:T(8,128)S(1)}) custom-call(s32[16]{0:T(128)S(1)} %stack.202.keep_ref, s32[16]{0:T(128)S(1)} %stack.219.slot_ref, bf16[48,3072]{1,0:T(8,128)(2,1)} %bitcast.77, bf16[48,3072]{1,0:T(8,128)(2,1)} %bitcast.79, bf16[96,3072]{1,0:T(8,128)(2,1)} %bitcast.87, bf16[96,3072]{1,0:T(8,128)(2,1)} %bitcast.93, ...), custom_call_target="tpu_custom_call" | custom-call | flops 7247757312 | bytes 16777216 | tf_op jit(solution)/shard_map/pallas_call | solution.py:121
  105.7 4.0 %collective-permute-start.18 = (f32[8,96,768]{2,1,0:T(8,128)S(1)}, f32[8,96,768]{2,1,0:T(8,128)S(1)}, u32[]{:S(2)}, u32[]{:S(2)}) collective-permute-start(f32[8,96,768]{2,1,0:T(8,128)S(1)} %get-tuple-element.74), channel_id=1, source_target_pairs={{0,1},{1,0},{2,3},{3,2},{4,5},{5,4},{6,7},{7,6},{8,9},{9,8},{10,11... | collective-permute-start | bytes 7077896 | tf_op jit(solution)/shard_map/ppermute | solution.py:200
  109.7 4.3 %collective-permute-done.18 = f32[8,96,768]{2,1,0:T(8,128)S(1)} collective-permute-done((f32[8,96,768]{2,1,0:T(8,128)S(1)}, f32[8,96,768]{2,1,0:T(8,128)S(1)}, u32[]{:S(2)}, u32[]{:S(2)}) %collective-permute-start.18) | collective-permute-done | bytes 2359328 | tf_op jit(solution)/shard_map/ppermute | solution.py:200
  114.0 1.7 %add.399 = f32[8,96,768]{2,1,0:T(8,128)} add(f32[8,96,768]{2,1,0:T(8,128)S(1)} %get-tuple-element.73, f32[8,96,768]{2,1,0:T(8,128)S(1)} %collective-permute-done.18) | non-fusion elementwise | flops 589824 | bytes 7077888 | tf_op jit(solution)/shard_map/add | solution.py:200
  115.8 4.7 %all-to-all-start = ((f32[8,96,768]{2,1,0:T(8,128)}), f32[8,96,768]{2,1,0:T(8,128)S(1)}, u32[]{:S(2)}, u32[]{:S(2)}) async-start(f32[8,96,768]{2,1,0:T(8,128)} %add.399), calls=%async_computation | async-start | bytes 4718592 | tf_op jit(solution)/shard_map/all_to_all | solution.py:201
  121.8 1.7 %copy-done = bf16[1536,768]{1,0:T(8,128)(2,1)S(1)} copy-done((bf16[1536,768]{1,0:T(8,128)(2,1)S(1)}, bf16[1536,768]{1,0:T(8,128)(2,1)}, u32[]{:S(2)}) %copy-start) | copy-done | bytes 2359320
  123.5 12.3 %shard_map.51 = bf16[768,3072]{1,0:T(8,128)(2,1)} custom-call(s32[32]{0:T(128)S(1)} %stack.185.slot_ref, bf16[16,96,768]{2,1,0:T(8,128)(2,1)S(1)} %bitcast.74, bf16[48,3072]{1,0:T(8,128)(2,1)} %bitcast.78, bf16[48,3072]{1,0:T(8,128)(2,1)} %bitcast.80, bf16[96,3072]{1,0:T(8,128)(2,1)} %bitcast.88, bf16[96,3072]{1,0:T(8,128)(2,1)} %bitcast.94, ...), custom_call_target="tpu_custom_call" | custom-call | flops 7247757312 | bytes 16777216 | tf_op jit(solution)/shard_map/pallas_call | solution.py:155
  135.8 13.7 %all-to-all-done = f32[8,96,768]{2,1,0:T(8,128)S(1)} async-done(((f32[8,96,768]{2,1,0:T(8,128)}), f32[8,96,768]{2,1,0:T(8,128)S(1)}, u32[]{:S(2)}, u32[]{:S(2)}) %all-to-all-start) | async-done | bytes 2359328 | tf_op jit(solution)/shard_map/all_to_all | solution.py:201
  (60 shorter events, 14.3 us)
Async XLA Ops:
  7.2 114.7 %all-gather.3.cloned.1.call-start = ((), (), s32[]{:S(2)}) async-start(), calls=%async_computation.1 | async-start | bytes 2506752 | tf_op jit(solution)/shard_map/all_gather | solution.py:184
  8.3 75.3 %copy-start.1 = (bf16[1,48,3072]{2,1,0:T(8,128)(2,1)}, bf16[1,48,3072]{2,1,0:T(8,128)(2,1)S(1)}, u32[]{:S(2)}) copy-start(bf16[1,48,3072]{2,1,0:T(8,128)(2,1)S(1)} %get-tuple-element.63) | copy-start | bytes 884740
  8.3 75.3 %copy-start.2 = (bf16[1,48,3072]{2,1,0:T(8,128)(2,1)}, bf16[1,48,3072]{2,1,0:T(8,128)(2,1)S(1)}, u32[]{:S(2)}) copy-start(bf16[1,48,3072]{2,1,0:T(8,128)(2,1)S(1)} %get-tuple-element.53) | copy-start | bytes 884740
  8.4 10.9 %collective-permute-start = (bf16[1,48,3072]{2,1,0:T(8,128)(2,1)S(1)}, bf16[1,48,3072]{2,1,0:T(8,128)(2,1)S(1)}, u32[]{:S(2)}, u32[]{:S(2)}) collective-permute-start(bf16[1,48,3072]{2,1,0:T(8,128)(2,1)S(1)} %get-tuple-element.53), channel_id=1, source_target_pairs={{0,16},{1,113},{2,18},{3,115},{4,20},{5,117},{6,22},{7,119},{8,24}... | collective-permute-start | bytes 884744 | tf_op jit(solution)/shard_map/ppermute | solution.py:55
  14.8 16.8 %collective-permute-start.5 = (bf16[1,48,3072]{2,1,0:T(8,128)(2,1)S(1)}, bf16[1,48,3072]{2,1,0:T(8,128)(2,1)S(1)}, u32[]{:S(2)}, u32[]{:S(2)}) collective-permute-start(bf16[1,48,3072]{2,1,0:T(8,128)(2,1)S(1)} %get-tuple-element.53), channel_id=1, source_target_pairs={{0,128},{16,144},{32,160},{48,176},{64,192},{80,208},{96,224},{112... | collective-permute-start | bytes 884744 | tf_op jit(solution)/shard_map/ppermute | solution.py:55
  17.6 11.3 %collective-permute-start.1 = (bf16[48,3072]{1,0:T(8,128)(2,1)S(1)}, bf16[48,3072]{1,0:T(8,128)(2,1)S(1)}, u32[]{:S(2)}, u32[]{:S(2)}) collective-permute-start(bf16[48,3072]{1,0:T(8,128)(2,1)S(1)} %get-tuple-element.77), channel_id=1, source_target_pairs={{0,128},{16,144},{32,160},{48,176},{64,192},{80,208},{96,224},{112... | collective-permute-start | bytes 884744 | tf_op jit(solution)/shard_map/ppermute | solution.py:55
  17.8 16.6 %collective-permute-start.10 = (bf16[1,48,3072]{2,1,0:T(8,128)(2,1)S(1)}, bf16[1,48,3072]{2,1,0:T(8,128)(2,1)S(1)}, u32[]{:S(2)}, u32[]{:S(2)}) collective-permute-start(bf16[1,48,3072]{2,1,0:T(8,128)(2,1)S(1)} %get-tuple-element.63), channel_id=1, source_target_pairs={{0,16},{1,113},{2,18},{3,115},{4,20},{5,117},{6,22},{7,119},{8,24}... | collective-permute-start | bytes 884744 | tf_op jit(solution)/shard_map/ppermute | solution.py:55
  19.3 64.4 %copy-start.3 = (bf16[1,48,3072]{2,1,0:T(8,128)(2,1)}, bf16[1,48,3072]{2,1,0:T(8,128)(2,1)S(1)}, u32[]{:S(2)}) copy-start(bf16[1,48,3072]{2,1,0:T(8,128)(2,1)S(1)} %collective-permute-done) | copy-start | bytes 884740
  28.9 9.0 %collective-permute-start.2 = (bf16[2,48,3072]{2,1,0:T(8,128)(2,1)S(1)}, bf16[2,48,3072]{2,1,0:T(8,128)(2,1)S(1)}, u32[]{:S(2)}, u32[]{:S(2)}) collective-permute-start(bf16[2,48,3072]{2,1,0:T(8,128)(2,1)S(1)} %pad_maximum_fusion), channel_id=1, source_target_pairs={{0,112},{1,17},{2,114},{3,19},{4,116},{5,21},{6,118},{7,23},{8,120... | collective-permute-start | bytes 1769480 | tf_op jit(solution)/shard_map/ppermute | solution.py:55
  28.9 7.1 %collective-permute-start.6 = (bf16[1,48,3072]{2,1,0:T(8,128)(2,1)S(1)}, bf16[1,48,3072]{2,1,0:T(8,128)(2,1)S(1)}, u32[]{:S(2)}, u32[]{:S(2)}) collective-permute-start(bf16[1,48,3072]{2,1,0:T(8,128)(2,1)S(1)} %collective-permute-done), channel_id=1, source_target_pairs={{0,128},{16,144},{32,160},{48,176},{64,192},{80,208},{96,224},{112... | collective-permute-start | bytes 884744 | tf_op jit(solution)/shard_map/ppermute | solution.py:55
  31.6 13.1 %collective-permute-start.14 = (bf16[1,48,3072]{2,1,0:T(8,128)(2,1)S(1)}, bf16[1,48,3072]{2,1,0:T(8,128)(2,1)S(1)}, u32[]{:S(2)}, u32[]{:S(2)}) collective-permute-start(bf16[1,48,3072]{2,1,0:T(8,128)(2,1)S(1)} %bitcast.81), channel_id=1, source_target_pairs={{0,16},{1,113},{2,18},{3,115},{4,20},{5,117},{6,22},{7,119},{8,24}... | collective-permute-start | bytes 884744 | tf_op jit(solution)/shard_map/ppermute | solution.py:55
  34.5 12.9 %collective-permute-start.11 = (bf16[2,48,3072]{2,1,0:T(8,128)(2,1)S(1)}, bf16[2,48,3072]{2,1,0:T(8,128)(2,1)S(1)}, u32[]{:S(2)}, u32[]{:S(2)}) collective-permute-start(bf16[2,48,3072]{2,1,0:T(8,128)(2,1)S(1)} %pad_maximum_fusion.1), channel_id=1, source_target_pairs={{0,112},{1,17},{2,114},{3,19},{4,116},{5,21},{6,118},{7,23},{8,120... | collective-permute-start | bytes 1769480 | tf_op jit(solution)/shard_map/ppermute | solution.py:55
  37.9 13.7 %collective-permute-start.7 = (bf16[2,48,3072]{2,1,0:T(8,128)(2,1)S(1)}, bf16[2,48,3072]{2,1,0:T(8,128)(2,1)S(1)}, u32[]{:S(2)}, u32[]{:S(2)}) collective-permute-start(bf16[2,48,3072]{2,1,0:T(8,128)(2,1)S(1)} %collective-permute-done.2), channel_id=1, source_target_pairs={{0,128},{16,144},{32,160},{48,176},{64,192},{80,208},{96,224},{112... | collective-permute-start | bytes 1769480 | tf_op jit(solution)/shard_map/ppermute | solution.py:55
  42.3 16.6 %collective-permute-start.3 = (bf16[2,48,3072]{2,1,0:T(8,128)(2,1)S(1)}, bf16[2,48,3072]{2,1,0:T(8,128)(2,1)S(1)}, u32[]{:S(2)}, u32[]{:S(2)}) collective-permute-start(bf16[2,48,3072]{2,1,0:T(8,128)(2,1)S(1)} %collective-permute-done.2), channel_id=1, source_target_pairs={{0,16},{1,113},{2,18},{3,115},{4,20},{5,117},{6,22},{7,119},{8,24}... | collective-permute-start | bytes 1769480 | tf_op jit(solution)/shard_map/ppermute | solution.py:55
  44.8 15.4 %collective-permute-start.15 = (bf16[2,48,3072]{2,1,0:T(8,128)(2,1)S(1)}, bf16[2,48,3072]{2,1,0:T(8,128)(2,1)S(1)}, u32[]{:S(2)}, u32[]{:S(2)}) collective-permute-start(bf16[2,48,3072]{2,1,0:T(8,128)(2,1)S(1)} %pad_maximum_fusion.2), channel_id=1, source_target_pairs={{0,112},{1,17},{2,114},{3,19},{4,116},{5,21},{6,118},{7,23},{8,120... | collective-permute-start | bytes 1769480 | tf_op jit(solution)/shard_map/ppermute | solution.py:55
  47.4 22.6 %collective-permute-start.12 = (bf16[2,48,3072]{2,1,0:T(8,128)(2,1)S(1)}, bf16[2,48,3072]{2,1,0:T(8,128)(2,1)}, u32[]{:S(2)}, u32[]{:S(2)}) collective-permute-start(bf16[2,48,3072]{2,1,0:T(8,128)(2,1)S(1)} %collective-permute-done.11), channel_id=1, source_target_pairs={{0,16},{1,113},{2,18},{3,115},{4,20},{5,117},{6,22},{7,119},{8,24}... | collective-permute-start | bytes 1769480 | tf_op jit(solution)/shard_map/ppermute | solution.py:55
  59.0 14.7 %collective-permute-start.8 = (bf16[2,48,3072]{2,1,0:T(8,128)(2,1)S(1)}, bf16[2,48,3072]{2,1,0:T(8,128)(2,1)S(1)}, u32[]{:S(2)}, u32[]{:S(2)}) collective-permute-start(bf16[2,48,3072]{2,1,0:T(8,128)(2,1)S(1)} %collective-permute-done.3), channel_id=1, source_target_pairs={{0,128},{16,144},{32,160},{48,176},{64,192},{80,208},{96,224},{112... | collective-permute-start | bytes 1769480 | tf_op jit(solution)/shard_map/ppermute | solution.py:55
  59.0 15.5 %collective-permute-start.4 = (bf16[2,48,3072]{2,1,0:T(8,128)(2,1)S(1)}, bf16[2,48,3072]{2,1,0:T(8,128)(2,1)}, u32[]{:S(2)}, u32[]{:S(2)}) collective-permute-start(bf16[2,48,3072]{2,1,0:T(8,128)(2,1)S(1)} %collective-permute-done.3), channel_id=1, source_target_pairs={{0,112},{1,17},{2,114},{3,19},{4,116},{5,21},{6,118},{7,23},{8,120... | collective-permute-start | bytes 1769480 | tf_op jit(solution)/shard_map/ppermute | solution.py:55
  60.2 22.5 %collective-permute-start.16 = (bf16[2,48,3072]{2,1,0:T(8,128)(2,1)S(1)}, bf16[2,48,3072]{2,1,0:T(8,128)(2,1)}, u32[]{:S(2)}, u32[]{:S(2)}) collective-permute-start(bf16[2,48,3072]{2,1,0:T(8,128)(2,1)S(1)} %collective-permute-done.15), channel_id=1, source_target_pairs={{0,16},{1,113},{2,18},{3,115},{4,20},{5,117},{6,22},{7,119},{8,24}... | collective-permute-start | bytes 1769480 | tf_op jit(solution)/shard_map/ppermute | solution.py:55
  70.0 15.6 %collective-permute-start.13 = (bf16[2,48,3072]{2,1,0:T(8,128)(2,1)}, bf16[2,48,3072]{2,1,0:T(8,128)(2,1)}, u32[]{:S(2)}, u32[]{:S(2)}) collective-permute-start(bf16[2,48,3072]{2,1,0:T(8,128)(2,1)} %collective-permute-done.12), channel_id=1, source_target_pairs={{0,112},{1,17},{2,114},{3,19},{4,116},{5,21},{6,118},{7,23},{8,120... | collective-permute-start | bytes 1769480 | tf_op jit(solution)/shard_map/ppermute | solution.py:55
  74.5 11.1 %collective-permute-start.9 = (bf16[2,48,3072]{2,1,0:T(8,128)(2,1)}, bf16[2,48,3072]{2,1,0:T(8,128)(2,1)}, u32[]{:S(2)}, u32[]{:S(2)}) collective-permute-start(bf16[2,48,3072]{2,1,0:T(8,128)(2,1)} %collective-permute-done.4), channel_id=1, source_target_pairs={{0,128},{16,144},{32,160},{48,176},{64,192},{80,208},{96,224},{112... | collective-permute-start | bytes 1769480 | tf_op jit(solution)/shard_map/ppermute | solution.py:55
  82.7 9.3 %collective-permute-start.17 = (bf16[2,48,3072]{2,1,0:T(8,128)(2,1)}, bf16[2,48,3072]{2,1,0:T(8,128)(2,1)}, u32[]{:S(2)}, u32[]{:S(2)}) collective-permute-start(bf16[2,48,3072]{2,1,0:T(8,128)(2,1)} %collective-permute-done.16), channel_id=1, source_target_pairs={{0,112},{1,17},{2,114},{3,19},{4,116},{5,21},{6,118},{7,23},{8,120... | collective-permute-start | bytes 1769480 | tf_op jit(solution)/shard_map/ppermute | solution.py:55
  105.7 8.3 %collective-permute-start.18 = (f32[8,96,768]{2,1,0:T(8,128)S(1)}, f32[8,96,768]{2,1,0:T(8,128)S(1)}, u32[]{:S(2)}, u32[]{:S(2)}) collective-permute-start(f32[8,96,768]{2,1,0:T(8,128)S(1)} %get-tuple-element.74), channel_id=1, source_target_pairs={{0,1},{1,0},{2,3},{3,2},{4,5},{5,4},{6,7},{7,6},{8,9},{9,8},{10,11... | collective-permute-start | bytes 7077896 | tf_op jit(solution)/shard_map/ppermute | solution.py:200
  115.8 33.7 %all-to-all-start = ((f32[8,96,768]{2,1,0:T(8,128)}), f32[8,96,768]{2,1,0:T(8,128)S(1)}, u32[]{:S(2)}, u32[]{:S(2)}) async-start(f32[8,96,768]{2,1,0:T(8,128)} %add.399), calls=%async_computation | async-start | bytes 4718592 | tf_op jit(solution)/shard_map/all_to_all | solution.py:201
  (12 other events, 382.4 us)
Sparse Core Ops, SparseCore 0:
  82.8 38.9 all-gather.2
